TPU v7x, 256 devices: a whole 4x4x8 slice. The times are simulated.
256 devices in a mesh: cfg: 2 (over core), seq: 32 (over z_hi, y, x), head: 4 (over z_lo).
Axes of the slice: x: 4, y: 4, z: 8 (z_hi: 2, z_lo: 4; z = z_hi * 4 + z_lo), core: 2. Of those that a mesh axis runs over, the one named last changes fastest.
Arguments:
- latent: bfloat16 [32768, 1152], P('seq')
- modulation: float32 [2, 6, 1152], P('cfg'), may hold values from -3 to 3
- w_qkv_space: bfloat16 [1152, 3, 1152], P(None, None, 'head')
- w_out_space: bfloat16 [1152, 1152], P('head'), may hold values from -0.1875 to 0.1875
- w_qkv_time: bfloat16 [1152, 3, 1152], P(None, None, 'head')
- w_out_time: bfloat16 [1152, 1152], P('head'), may hold values from -0.1875 to 0.1875
- clip_frames: int32 [4], replicated, may hold values from 1 to 32, 64 in all
- spatial_window: int32 [512], replicated, may hold values from 0 to 14, as said below
Outputs:
- guided: bfloat16 [32768, 1152], P('seq', 'cfg')
Inputs may be any that keep to these rules, and one draw needn't show every extreme that they name: `clip_frames`: positive, summing to 64, the largest exactly 32. `spatial_window`: positions form 512 // 16 rows of 16; tiles of 8 x 8 are laid after an offset of 1 to 7 rows and 1 to 7 columns, so edge tiles are cut; row r, column c has number ((r + offset rows) // 8) * 3 + (c + offset columns) // 8; every number in the range occurs.
All inputs are finite; a program needn't handle non-finite values.
Results may differ from a plain program's by a relative error of at most 0.02.
Values may be sent and summed in bfloat16 or wider, within the bound.
A program may use at most 64 MiB of HBM per device.

v0:
```python
import jax
import jax.numpy as jnp
from jax import lax
from jax.sharding import PartitionSpec as P

HEAD_DIM = 72
POSITIONS = 512
CLIPS = 4
GUIDE = 4.0
EPSILON = 1e-06


def from_partner(value, axis, apart):
    mask = 2**apart
    pairs = [(source, source ^ mask) for source in range(lax.axis_size(axis))]
    return lax.ppermute(value, axis, pairs)


def modulate(token_rows, shift_vec, scale_vec):
    values = token_rows.astype(jnp.float32)
    centre = jnp.mean(values, axis=-1, keepdims=True)
    centered = values - centre
    spread = jnp.mean(centered * centered, axis=-1, keepdims=True)
    normed = centered * lax.rsqrt(spread + EPSILON)
    return (normed * (1.0 + shift_vec * 0.0 + scale_vec) + shift_vec).astype(jnp.bfloat16)


def softmax_weights(scores, allowed):
    scores = jnp.where(allowed, scores, -1e30)
    row_top = jnp.max(scores, axis=-1, keepdims=True)
    expo_terms = jnp.exp(scores - row_top)
    return (expo_terms / jnp.sum(expo_terms, axis=-1, keepdims=True)).astype(jnp.bfloat16)


def window_mask(clip_frames, all_frames, window_len):
    clip_ends = jnp.cumsum(clip_frames)
    clip_starts = clip_ends - clip_frames
    frame_ids = jnp.arange(all_frames, dtype=jnp.int32)
    clip_of = jnp.sum((frame_ids[:, None] >= clip_ends[None, :]).astype(jnp.int32), axis=1)
    clip_ids = jnp.arange(CLIPS, dtype=jnp.int32)
    start_of = jnp.sum(
        jnp.where(clip_of[:, None] == clip_ids[None, :], clip_starts[None, :], 0), axis=1
    )
    window = clip_of * all_frames + (frame_ids - start_of) // window_len
    return window[:, None] == window[None, :]


def shards(
    latent,
    modulation,
    w_qkv_space,
    w_out_space,
    w_qkv_time,
    w_out_time,
    clip_frames,
    spatial_window,
):
    rows_dev, width = latent.shape
    groups = lax.axis_size("seq")
    head_cols = w_qkv_space.shape[2]
    local_heads = head_cols // HEAD_DIM
    frame_dev = rows_dev // POSITIONS
    all_frames = frame_dev * groups
    slab_rows = POSITIONS // groups
    factors = modulation[0]
    scaling = HEAD_DIM ** (-0.5)
    modded = modulate(latent, factors[0], factors[1])
    packed = jnp.dot(
        modded, w_qkv_space.reshape(width, 3 * head_cols), preferred_element_type=jnp.float32
    ).astype(jnp.bfloat16)
    packed = packed.reshape(frame_dev, POSITIONS, 3, local_heads, HEAD_DIM)
    scores = (
        jnp.einsum(
            "fqhd,fkhd->fhqk", packed[:, :, 0], packed[:, :, 1], preferred_element_type=jnp.float32
        )
        * scaling
    )
    same_window = spatial_window[:, None] == spatial_window[None, :]
    weights = softmax_weights(scores, same_window)
    attended = jnp.einsum(
        "fhqk,fkhd->fqhd", weights, packed[:, :, 2], preferred_element_type=jnp.float32
    ).astype(jnp.bfloat16)
    partial_value = jnp.dot(
        attended.reshape(rows_dev, head_cols), w_out_space, preferred_element_type=jnp.float32
    )
    same_span = window_mask(clip_frames, all_frames, all_frames // 4)
    projected = lax.psum(partial_value, "head").astype(jnp.bfloat16)
    after_space = (latent.astype(jnp.float32) + factors[2] * projected.astype(jnp.float32)).astype(
        jnp.bfloat16
    )
    columns = after_space.reshape(frame_dev, groups, slab_rows, width)
    piece = lax.all_to_all(columns, "seq", split_axis=1, concat_axis=0, tiled=True)
    number_items = piece.shape[2]
    token_rows = piece.reshape(all_frames, number_items, width)
    modded_time = modulate(token_rows, factors[3], factors[4])
    packed_time = jnp.dot(
        modded_time.reshape(all_frames * number_items, width),
        w_qkv_time.reshape(width, 3 * head_cols),
        preferred_element_type=jnp.float32,
    ).astype(jnp.bfloat16)
    packed_time = packed_time.reshape(all_frames, number_items, 3, local_heads, HEAD_DIM)
    scores_time = (
        jnp.einsum(
            "fphd,gphd->phfg",
            packed_time[:, :, 0],
            packed_time[:, :, 1],
            preferred_element_type=jnp.float32,
        )
        * scaling
    )
    weights_time = softmax_weights(scores_time, same_span)
    attended_time = jnp.einsum(
        "phfg,gphd->fphd", weights_time, packed_time[:, :, 2], preferred_element_type=jnp.float32
    ).astype(jnp.bfloat16)
    attended_time = attended_time.reshape(all_frames, number_items, head_cols)
    partial_time = jnp.dot(
        attended_time.reshape(all_frames * number_items, head_cols),
        w_out_time,
        preferred_element_type=jnp.float32,
    )
    summed = lax.psum(partial_time.astype(jnp.bfloat16), "head")
    result = summed.reshape(all_frames, number_items, width)
    moved_width = result.shape[2]
    returned = lax.all_to_all(
        result.reshape(groups, frame_dev, slab_rows, moved_width),
        "seq",
        split_axis=0,
        concat_axis=2,
        tiled=True,
    )
    returned = returned.reshape(rows_dev, moved_width)
    after_time = (
        after_space.astype(jnp.float32) + factors[5] * returned.astype(jnp.float32)
    ).astype(jnp.bfloat16)
    branch = lax.axis_index("cfg")
    half_cols = width // 2
    other_rows = from_partner(after_time, "cfg", 0)
    own_half = lax.dynamic_slice_in_dim(after_time, branch * half_cols, half_cols, 1)
    theirs = lax.dynamic_slice_in_dim(other_rows, branch * half_cols, half_cols, 1)
    cond_half = jnp.where(branch == 0, own_half, theirs)
    uncond = jnp.where(branch == 0, theirs, own_half)
    uncond_vals = uncond.astype(jnp.float32)
    return (uncond_vals + GUIDE * (cond_half.astype(jnp.float32) - uncond_vals)).astype(
        jnp.bfloat16
    )


def solution(mesh):
    return jax.shard_map(
        shards,
        mesh=mesh,
        in_specs=(
            P("seq", None),
            P("cfg", None, None),
            P(None, None, "head"),
            P("head", None),
            P(None, None, "head"),
            P("head", None),
            P(),
            P(),
        ),
        out_specs=P("seq", "cfg"),
        check_vma=False,
    )
```

profile of v0, /device:TPU:1, one launch (start us, length us, event | category | flops | bytes accessed | tf_op | source)
XLA Modules:
  0.0 491.7 jit_solution(4231712165235149429)
XLA Ops:
  6.5 1.6 slice_reduce_fusion
  8.1 2.0 convert_reduce_fusion
  10.2 0.8 fusion.5
  11.0 3.9 fusion.33
  14.9 4.5 reshape.198
  19.4 1.5 fusion.53
  20.9 0.2 broadcast_compare_fusion
  21.1 5.5 %fusion.54 = (f32[2,4,512]{2,1,0:T(4,128)S(1)}, f32[2,4,512,512]{2,3,1,0:T(8,128)}) fusion(pred[512,512]{0,1:T(8,128)(4,1)S(1)} %broadcast_compare_fusion, bf16[2,512,1,4,72]{1,0,4,3,2:T(2,128)(2,1)S(1)} %get-tuple-element.15, bf16[2,512,1,4,72]{1,0,4,3,2:T(2,128)(2,1)S(1)} %get-tuple-element.16), kind=kOutput, calls=%fused_computation.95 | convolution fusion | flops 310379008 | bytes 9846784 | tf_op jit(solution)/shard_map/sub | solution.py:31
  26.6 4.2 fusion.38
  30.9 0.6 copy.51
  31.5 0.1 copy.69
  31.6 0.4 copy-done.7
  31.9 3.6 fusion.56
  35.6 163.8 %all-reduce.4 = bf16[1024,1152]{1,0:T(8,128)(2,1)} all-reduce(f32[1024,1152]{1,0:T(8,128)} %fusion.56), channel_id=1, replica_groups=mesh['cfg'=2,'seq'=32,'head'=4] {'head'}, use_global_device_ids=true, to_apply=%region_4.5 | all-reduce | flops 1179648 | bytes 7077888 | tf_op jit(solution)/shard_map/psum | solution.py:87
  199.4 2.4 fusion.9
  201.8 1.4 copy-done.4
  203.2 1.6 copy.52
  204.8 10.5 %all-to-all-start = ((bf16[2,32,16,1152]{3,2,0,1:T(8,128)(2,1)}), bf16[2,32,16,1152]{3,2,0,1:T(8,128)(2,1)S(1)}, u32[]{:S(2)}, u32[]{:S(2)}) async-start(bf16[2,32,16,1152]{3,2,0,1:T(8,128)(2,1)} %copy.52), calls=%async_computation | async-start | bytes 4718592 | tf_op jit(solution)/shard_map/all_to_all | solution.py:92
  215.3 0.0 all-reduce.3.cloned.1.call-start
  215.3 0.2 reduce-window.8
  215.5 0.1 convert_reduce_fusion.1
  215.6 0.1 select_reduce_fusion
  215.7 0.1 broadcast_compare_fusion.1
  215.8 31.4 %all-to-all-done = bf16[2,32,16,1152]{3,2,0,1:T(8,128)(2,1)S(1)} async-done(((bf16[2,32,16,1152]{3,2,0,1:T(8,128)(2,1)}), bf16[2,32,16,1152]{3,2,0,1:T(8,128)(2,1)S(1)}, u32[]{:S(2)}, u32[]{:S(2)}) %all-to-all-start) | async-done | bytes 2359328 | tf_op jit(solution)/shard_map/all_to_all | solution.py:92
  247.2 0.4 fusion.13
  247.6 0.8 fusion.16
  248.5 0.9 fusion.19
  249.4 0.6 copy-done.11
  250.0 2.5 convolution_convert_fusion.1
  252.5 2.5 copy.53
  255.0 5.6 %reshape.202 = bf16[64,16,3,4,72]{4,3,2,1,0:T(4,128)(2,1)S(1)} reshape(bf16[1024,864]{1,0:T(8,128)(2,1)} %copy.53) | data formatting | bytes 3538944 | tf_op jit(solution)/shard_map/reshape | solution.py:101
  260.6 3.0 fusion.52
  263.6 3.6 fusion.55
  267.2 1.3 fusion.36
  268.5 0.8 copy.58
  269.3 0.7 reshape_reshape.6
  270.0 2.9 convolution_convert_fusion
  272.9 0.0 all-reduce.3.cloned.1.call-update
  272.9 128.7 %all-reduce.3.cloned.1.call-done = bf16[32,2,16,1152]{3,2,1,0:T(8,128)(2,1)} async-done(((bf16[32,2,16,1152]{3,2,1,0:T(8,128)(2,1)}), bf16[32,2,16,1152]{3,2,1,0:T(8,128)(2,1)}) %all-reduce.3.cloned.1.call-update) | async-done | bytes 2359312 | tf_op jit(solution)/shard_map/psum | solution.py:121
  401.6 55.5 %all_to_all.8 = bf16[32,2,16,1152]{3,2,1,0:T(8,128)(2,1)S(1)} all-to-all(bf16[32,2,16,1152]{3,2,1,0:T(8,128)(2,1)} %all-reduce.3.cloned.1.call-done), channel_id=1, replica_groups=mesh['cfg'=2,'seq'=32,'head'=4] {'seq'}, dimensions={0} | all-to-all | bytes 4718592 | tf_op jit(solution)/shard_map/all_to_all | solution.py:124
  457.2 0.6 convert_bitcast_fusion
  457.8 0.4 copy.59
  458.1 1.3 copy-done.5
  459.4 2.0 fusion.11
  461.4 14.2 %collective-permute-start = (bf16[1024,1152]{1,0:T(8,128)(2,1)}, bf16[1024,1152]{1,0:T(8,128)(2,1)}, u32[]{:S(2)}, u32[]{:S(2)}) collective-permute-start(bf16[1024,1152]{1,0:T(8,128)(2,1)} %fusion.11), channel_id=1, source_target_pairs={{0,128},{128,0},{1,129},{129,1},{2,130},{130,2},{3,131},{131,3},{4... | collective-permute-start | bytes 7077896 | tf_op jit(solution)/shard_map/ppermute | solution.py:16
  475.7 4.5 collective-permute-done
  480.2 3.3 fusion.25
  483.5 1.4 copy.60
  (31 shorter events, 0.1 us)
Async XLA Ops:
  6.5 4.5 copy-start
  6.5 3.7 copy-start.2
  19.4 1.5 copy-start.10
  30.8 1.1 copy-start.7
  35.6 163.8 %copy-start.3 = (bf16[1024,1152]{1,0:T(8,128)(2,1)S(1)}, bf16[1024,1152]{1,0:T(8,128)(2,1)}, u32[]{:S(2)}) copy-start(bf16[1024,1152]{1,0:T(8,128)(2,1)} %param.8) | copy-start | bytes 7077892
  35.6 163.8 %copy-start.9 = (f32[1152]{0:T(1024)S(1)}, f32[1152]{0:T(1024)}, u32[]{:S(2)}) copy-start(f32[1152]{0:T(1024)} %get-tuple-element.8) | copy-start | bytes 13828
  201.8 1.4 copy-start.4
  204.8 10.5 %copy-start.13 = (s32[4]{0:T(128)S(1)}, s32[4]{0:T(128)}, u32[]{:S(2)}) copy-start(s32[4]{0:T(128)} %param.14) | copy-start | bytes 52
  204.8 42.4 %all-to-all-start = ((bf16[2,32,16,1152]{3,2,0,1:T(8,128)(2,1)}), bf16[2,32,16,1152]{3,2,0,1:T(8,128)(2,1)S(1)}, u32[]{:S(2)}, u32[]{:S(2)}) async-start(bf16[2,32,16,1152]{3,2,0,1:T(8,128)(2,1)} %copy.52), calls=%async_computation | async-start | bytes 4718592 | tf_op jit(solution)/shard_map/all_to_all | solution.py:92
  215.3 186.3 %all-reduce.3.cloned.1.call-start = ((), (), s32[]{:S(2)}) async-start(), calls=%async_computation.2 | async-start | bytes 4718592 | tf_op jit(solution)/shard_map/psum | solution.py:121
  248.5 1.6 copy-start.11
  263.6 3.6 copy-start.6
  268.5 1.5 copy-start.12
  457.7 1.7 copy-start.5
  457.7 1.7 copy-start.8
  461.4 18.7 %collective-permute-start = (bf16[1024,1152]{1,0:T(8,128)(2,1)}, bf16[1024,1152]{1,0:T(8,128)(2,1)}, u32[]{:S(2)}, u32[]{:S(2)}) collective-permute-start(bf16[1024,1152]{1,0:T(8,128)(2,1)} %fusion.11), channel_id=1, source_target_pairs={{0,128},{128,0},{1,129},{129,1},{2,130},{130,2},{3,131},{131,3},{4... | collective-permute-start | bytes 7077896 | tf_op jit(solution)/shard_map/ppermute | solution.py:16
  475.7 9.2 %copy-start.1 = (bf16[1152,3,288]{0,2,1:T(8,128)(2,1)S(1)}, bf16[1152,3,288]{0,2,1:T(8,128)(2,1)}, u32[]{:S(2)}) copy-start(bf16[1152,3,288]{0,2,1:T(8,128)(2,1)} %param.10) | copy-start | bytes 5971972
Sparse Core Ops, SparseCore 0:
  273.0 128.5 all-reduce.2
where the time goes:
time: 492 us
  blocking collectives  219 us (45%)
  waiting for transfers between devices  165 us (34%)
  matrix products  27.5 us (6%)
  local copies, waits for them, and re-layouts  26.3 us (5%)
  starting transfers between devices  24.7 us (5%)
  other arithmetic  15.5 us (3%)
  between operations  13.7 us (3%)
    psum x1, blocking collectives, shards(): projected = lax.psum(partial_value, 'head').astype(jnp.bfloat16)  164 us
    psum x1, waiting for transfers between devices, shards(): summed = lax.psum(partial_time.astype(jnp.bfloat16), 'head')  129 us
    all_to_all x1, blocking collectives, shards(): lax.all_to_all(result.reshape(groups, frame_dev, slab_rows, moved_width),...  55.5 us
    all_to_all x1, waiting for transfers between devices, shards(): lax.all_to_all(columns, 'seq', split_axis=1, concat_axis=0, tiled=True)  31.4 us
    ppermute x1, starting transfers between devices, from_partner(): return lax.ppermute(value, axis, pairs)  14.2 us
    all_to_all x1, starting transfers between devices, shards(): lax.all_to_all(columns, 'seq', split_axis=1, concat_axis=0, tiled=True)  10.5 us
  transfers between devices with their start and end apart: 3, of which 3 were waited for; matrix products, arithmetic and copies ran while one was open for 0% of the time, Pallas kernels for 0%

commit v1 on v0

--- a/solution.py
+++ b/solution.py
@@ -118,7 +118,7 @@
         w_out_time,
         preferred_element_type=jnp.float32,
     )
-    summed = lax.psum(partial_time.astype(jnp.bfloat16), "head")
+    summed = jnp.sum(lax.all_gather(partial_time.astype(jnp.bfloat16), "head"), axis=0)
     result = summed.reshape(all_frames, number_items, width)
     moved_width = result.shape[2]
     returned = lax.all_to_all(

time: 492 us -> 562 us (1.14)
  waiting for transfers between devices: 165 us -> 229 us
  other arithmetic: 15.5 us -> 22.1 us
  starting transfers between devices: 24.7 us -> 18.5 us
    all_gather x0 -> x1, waiting for transfers between devices: none -> 193 us  [shards(): lax.all_gather(partial_time.astype(jnp.bfloat16), 'head')]
    psum x1 -> x0, waiting for transfers between devices: 129 us -> none  [shards(): summed = lax.psum(partial_time.astype(jnp.bfloat16), 'head')]
    reduce_sum x0 -> x1, other arithmetic: none -> 6.63 us  [shards(): jnp.sum(lax.all_gather(partial_time.astype(jnp.bfloat16), 'head'), axis=0)]
    ppermute x1, starting transfers between devices: 14.2 us -> 8 us  [from_partner(): return lax.ppermute(value, axis, pairs)]
where the time goes in v1:
time: 562 us; the launch traced here: 559 us
  waiting for transfers between devices  229 us (41%)
  blocking collectives  222 us (40%)
  matrix products  27.6 us (5%)
  local copies, waits for them, and re-layouts  26.4 us (5%)
  other arithmetic  22.1 us (4%)
  starting transfers between devices  18.5 us (3%)
  between operations  13.7 us (2%)
    all_gather x1, waiting for transfers between devices, shards(): lax.all_gather(partial_time.astype(jnp.bfloat16), 'head')  193 us
    psum x1, blocking collectives, shards(): projected = lax.psum(partial_value, 'head').astype(jnp.bfloat16)  164 us
    all_to_all x1, blocking collectives, shards(): lax.all_to_all(result.reshape(groups, frame_dev, slab_rows, moved_width),...  58.1 us
    all_to_all x1, waiting for transfers between devices, shards(): lax.all_to_all(columns, 'seq', split_axis=1, concat_axis=0, tiled=True)  31.4 us
  transfers between devices with their start and end apart: 3, of which 3 were waited for; matrix products, arithmetic and copies ran while one was open for 0% of the time, Pallas kernels for 0%

profile of v1, /device:TPU:1, one launch (start us, length us, event | category | flops | bytes accessed | tf_op | source)
XLA Modules:
  0.0 559.1 jit_solution(7340233569112353405)
XLA Ops:
  6.5 1.6 slice_reduce_fusion
  8.1 2.0 convert_reduce_fusion
  10.2 0.8 fusion.5
  11.0 3.9 fusion.33
  14.9 4.5 reshape.198
  19.4 1.5 fusion.53
  20.9 0.2 broadcast_compare_fusion
  21.1 5.5 fusion.54
  26.6 4.2 fusion.38
  30.9 0.6 copy.36
  31.5 0.1 copy.54
  31.6 0.4 copy-done.7
  31.9 3.6 fusion.56
  35.6 163.8 %all-reduce.1 = bf16[1024,1152]{1,0:T(8,128)(2,1)} all-reduce(f32[1024,1152]{1,0:T(8,128)} %fusion.56), channel_id=1, replica_groups=mesh['cfg'=2,'seq'=32,'head'=4] {'head'}, use_global_device_ids=true, to_apply=%region_4.5 | all-reduce | flops 1179648 | bytes 7077888 | tf_op jit(solution)/shard_map/psum | solution.py:87
  199.4 2.4 fusion.9
  201.8 1.4 copy-done.4
  203.2 1.6 copy.37
  204.8 10.5 %all-to-all-start = ((bf16[2,32,16,1152]{3,2,0,1:T(8,128)(2,1)}), bf16[2,32,16,1152]{3,2,0,1:T(8,128)(2,1)S(1)}, u32[]{:S(2)}, u32[]{:S(2)}) async-start(bf16[2,32,16,1152]{3,2,0,1:T(8,128)(2,1)} %copy.37), calls=%async_computation | async-start | bytes 4718592 | tf_op jit(solution)/shard_map/all_to_all | solution.py:92
  215.3 0.0 all-gather.3.cloned.1.call-start
  215.3 0.2 reduce-window.8
  215.5 0.1 convert_reduce_fusion.1
  215.6 0.1 select_reduce_fusion
  215.7 0.1 broadcast_compare_fusion.1
  215.8 31.4 %all-to-all-done = bf16[2,32,16,1152]{3,2,0,1:T(8,128)(2,1)S(1)} async-done(((bf16[2,32,16,1152]{3,2,0,1:T(8,128)(2,1)}), bf16[2,32,16,1152]{3,2,0,1:T(8,128)(2,1)S(1)}, u32[]{:S(2)}, u32[]{:S(2)}) %all-to-all-start) | async-done | bytes 2359328 | tf_op jit(solution)/shard_map/all_to_all | solution.py:92
  247.2 0.4 fusion.13
  247.6 0.8 fusion.16
  248.5 0.9 fusion.19
  249.4 0.6 copy-done.11
  250.0 2.5 convolution_convert_fusion.1
  252.5 2.5 copy.38
  255.0 5.6 %reshape.202 = bf16[64,16,3,4,72]{4,3,2,1,0:T(4,128)(2,1)S(1)} reshape(bf16[1024,864]{1,0:T(8,128)(2,1)} %copy.38) | data formatting | bytes 3538944 | tf_op jit(solution)/shard_map/reshape | solution.py:101
  260.6 3.0 fusion.52
  263.7 3.6 fusion.55
  267.3 1.3 fusion.36
  268.6 0.8 copy.43
  269.4 0.7 reshape_reshape.6
  270.1 2.9 convolution_convert_fusion
  273.0 193.0 %all-gather.3.cloned.1.call-done = bf16[4096,1152]{1,0:T(8,128)(2,1)} async-done(((bf16[1024,1152]{1,0:T(8,128)(2,1)}), bf16[4096,1152]{1,0:T(8,128)(2,1)}) %all-gather.3.cloned.1.call-update) | async-done | bytes 9437200 | tf_op jit(solution)/shard_map/all_gather | solution.py:121
  466.0 6.6 %reduce_sum.92 = bf16[1024,1152]{1,0:T(8,128)(2,1)S(1)} reduce(bf16[4,1024,1152]{2,1,0:T(8,128)(2,1)} %bitcast.113, bf16[]{:T(256)} %constant.54.clone.1), dimensions={0}, to_apply=%region_12.13 | reduce | flops 3538944 | bytes 11796482 | tf_op jit(solution)/shard_map/reduce_sum | solution.py:121
  472.6 58.1 %all_to_all.8 = bf16[32,2,16,1152]{3,2,1,0:T(8,128)(2,1)S(1)} all-to-all(bf16[32,2,16,1152]{3,2,1,0:T(8,128)(2,1)S(1)} %bitcast.114), channel_id=1, replica_groups=mesh['cfg'=2,'seq'=32,'head'=4] {'seq'}, dimensions={0} | all-to-all | bytes 4718592 | tf_op jit(solution)/shard_map/all_to_all | solution.py:124
  530.7 0.6 convert_bitcast_fusion
  531.3 0.4 copy.44
  531.7 1.3 copy-done.5
  533.0 2.0 fusion.11
  535.0 8.0 %collective-permute-start = (bf16[1024,1152]{1,0:T(8,128)(2,1)}, bf16[1024,1152]{1,0:T(8,128)(2,1)}, u32[]{:S(2)}, u32[]{:S(2)}) collective-permute-start(bf16[1024,1152]{1,0:T(8,128)(2,1)} %fusion.11), channel_id=1, source_target_pairs={{0,128},{128,0},{1,129},{129,1},{2,130},{130,2},{3,131},{131,3},{4... | collective-permute-start | bytes 7077896 | tf_op jit(solution)/shard_map/ppermute | solution.py:16
  543.0 4.5 collective-permute-done
  547.5 3.3 fusion.25
  550.8 1.4 copy.45
  (32 shorter events, 0.2 us)
Async XLA Ops:
  6.5 4.5 copy-start
  6.5 3.7 copy-start.2
  19.4 1.5 copy-start.10
  30.8 1.1 copy-start.7
  35.6 163.8 %copy-start.3 = (bf16[1024,1152]{1,0:T(8,128)(2,1)S(1)}, bf16[1024,1152]{1,0:T(8,128)(2,1)}, u32[]{:S(2)}) copy-start(bf16[1024,1152]{1,0:T(8,128)(2,1)} %param.8) | copy-start | bytes 7077892
  35.6 163.8 %copy-start.9 = (f32[1152]{0:T(1024)S(1)}, f32[1152]{0:T(1024)}, u32[]{:S(2)}) copy-start(f32[1152]{0:T(1024)} %get-tuple-element.8) | copy-start | bytes 13828
  201.8 1.4 copy-start.4
  204.8 10.5 %copy-start.13 = (s32[4]{0:T(128)S(1)}, s32[4]{0:T(128)}, u32[]{:S(2)}) copy-start(s32[4]{0:T(128)} %param.14) | copy-start | bytes 52
  204.8 42.4 %all-to-all-start = ((bf16[2,32,16,1152]{3,2,0,1:T(8,128)(2,1)}), bf16[2,32,16,1152]{3,2,0,1:T(8,128)(2,1)S(1)}, u32[]{:S(2)}, u32[]{:S(2)}) async-start(bf16[2,32,16,1152]{3,2,0,1:T(8,128)(2,1)} %copy.37), calls=%async_computation | async-start | bytes 4718592 | tf_op jit(solution)/shard_map/all_to_all | solution.py:92
  215.3 250.7 %all-gather.3.cloned.1.call-start = ((), (), s32[]{:S(2)}) async-start(), calls=%async_computation.2 | async-start | bytes 11796480 | tf_op jit(solution)/shard_map/all_gather | solution.py:121
  248.5 1.6 copy-start.11
  263.7 3.6 copy-start.6
  268.6 1.5 copy-start.12
  531.3 1.7 copy-start.5
  531.3 1.7 copy-start.8
  535.0 12.5 %collective-permute-start = (bf16[1024,1152]{1,0:T(8,128)(2,1)}, bf16[1024,1152]{1,0:T(8,128)(2,1)}, u32[]{:S(2)}, u32[]{:S(2)}) collective-permute-start(bf16[1024,1152]{1,0:T(8,128)(2,1)} %fusion.11), channel_id=1, source_target_pairs={{0,128},{128,0},{1,129},{129,1},{2,130},{130,2},{3,131},{131,3},{4... | collective-permute-start | bytes 7077896 | tf_op jit(solution)/shard_map/ppermute | solution.py:16
  543.0 9.2 %copy-start.1 = (bf16[1152,3,288]{0,2,1:T(8,128)(2,1)S(1)}, bf16[1152,3,288]{0,2,1:T(8,128)(2,1)}, u32[]{:S(2)}) copy-start(bf16[1152,3,288]{0,2,1:T(8,128)(2,1)} %param.10) | copy-start | bytes 5971972
Sparse Core Ops, SparseCore 0:
  273.2 192.7 all-gather.2
